TPU v7x, 128 devices: a whole 4x4x4 slice. The times are simulated.
128 devices in a mesh: section: 2 (over x_lo), dp: 8 (over x_hi, y), tensor: 8 (over z, core).
Axes of the slice: x: 4 (x_hi: 2, x_lo: 2; x = x_hi * 2 + x_lo), y: 4, z: 4, core: 2. Of those that a mesh axis runs over, the one named last changes fastest.
Arguments:
- tokens: bfloat16 [2048, 8192], P('dp', ('section', 'tensor')), may hold values from -6 to 6
- segment_ids: int32 [8, 256], P('dp'), may hold values from 0 to 3, never falling along the last dimension, each value on 1 to 128 neighbouring positions
- gain_attn: float32 [8192], replicated, may hold values from 0.1 to 1.9
- w_query: bfloat16 [8192, 4096], P(None, ('section', 'tensor')), may hold values from -0.06629126 to 0.06629126
- w_key: bfloat16 [8192, 4096], P(None, ('section', 'tensor')), may hold values from -0.06629126 to 0.06629126
- w_value: bfloat16 [8192, 4096], P(None, ('section', 'tensor')), may hold values from -0.0625 to 0.0625
- w_output: bfloat16 [4096, 8192], P(('section', 'tensor')), may hold values from -0.09375 to 0.09375
- gain_ffn: float32 [8192], replicated, may hold values from 0.1 to 1.9
- w_up: bfloat16 [8192, 16384], P(('section', 'tensor'), 'dp'), may hold values from -0.0625 to 0.0625
- w_down: bfloat16 [16384, 8192], P('dp', ('section', 'tensor')), may hold values from -0.046875 to 0.046875
Outputs:
- layer_out: bfloat16 [2048, 8192], P('dp', ('section', 'tensor'))
Inputs may be any that keep to these rules, and one draw needn't show every extreme that they name: `segment_ids`: segment numbers never fall along a replica's tokens; each segment holds 1 to 128 tokens.
All inputs are finite; a program needn't handle non-finite values.
Results may differ from a plain program's by a relative error of at most 0.023.
Values may be sent and summed in bfloat16 or wider, within the bound.
A program may use at most 128 MiB of HBM per device.

v0:
```python
import jax
import jax.numpy as jnp
from jax import lax
from jax.sharding import PartitionSpec as P

HD = 128


def layer_norm(values, gain):
    mean = jnp.mean(values, axis=-1, keepdims=True)
    second = jnp.mean(values * values, axis=-1, keepdims=True)
    return (values - mean) * lax.rsqrt(second - mean * mean + 1e-05) * gain


def per_device(
    tokens, segment_ids, gain_attn, w_query, w_key, w_value, w_output, gain_ffn, w_up, w_down
):
    tok_rows = tokens.shape[0]
    width = gain_attn.shape[0]
    groups = lax.axis_size(("section", "tensor"))
    share = width // groups
    first_col = lax.axis_index(("section", "tensor")) * share
    whole = lax.all_gather(tokens, ("section", "tensor"), axis=1, tiled=True)
    normed = layer_norm(whole.astype(jnp.float32), gain_attn).astype(jnp.bfloat16)
    local_heads = w_query.shape[1] // HD
    query = jnp.dot(normed, w_query, preferred_element_type=jnp.float32).astype(jnp.bfloat16)
    key = jnp.dot(normed, w_key, preferred_element_type=jnp.float32).astype(jnp.bfloat16)
    value = jnp.dot(normed, w_value, preferred_element_type=jnp.float32).astype(jnp.bfloat16)
    query = query.reshape(tok_rows, local_heads, HD)
    key = key.reshape(tok_rows, local_heads, HD)
    value = value.reshape(tok_rows, local_heads, HD)
    scores = jnp.einsum("qhd,khd->hqk", query, key, preferred_element_type=jnp.float32) * HD ** (
        -0.5
    )
    position = jnp.arange(tok_rows)
    segment_row = segment_ids[0]
    keep = jnp.logical_and(
        position[:, None] >= position[None, :], segment_row[:, None] == segment_row[None, :]
    )
    scores = jnp.where(keep[None], scores, -1e30)
    top = jnp.max(scores, axis=-1, keepdims=True)
    expo = jnp.exp(scores - top)
    probs = (expo / jnp.sum(expo, axis=-1, keepdims=True)).astype(jnp.bfloat16)
    context = jnp.einsum("hqk,khd->qhd", probs, value, preferred_element_type=jnp.float32)
    context = context.astype(jnp.bfloat16).reshape(tok_rows, local_heads * HD)
    partial_out = jnp.dot(context, w_output, preferred_element_type=jnp.float32)
    summed = lax.psum(partial_out.astype(jnp.bfloat16), ("section", "tensor")).astype(jnp.float32)
    resid_full = (whole.astype(jnp.float32) + summed).astype(jnp.bfloat16)
    normed_full = layer_norm(resid_full.astype(jnp.float32), gain_ffn).astype(jnp.bfloat16)
    normed_ffn = lax.dynamic_slice_in_dim(normed_full, first_col, share, 1)
    resid_mid = lax.dynamic_slice_in_dim(resid_full, first_col, share, 1)
    gathered = lax.all_gather(normed_ffn, "dp", axis=0, tiled=True)
    pre_act = lax.psum_scatter(
        jnp.dot(gathered, w_up, preferred_element_type=jnp.float32).astype(jnp.bfloat16),
        ("section", "tensor"),
        scatter_dimension=0,
        tiled=True,
    ).astype(jnp.float32)
    activated = jax.nn.gelu(pre_act, approximate=True).astype(jnp.bfloat16)
    partial_down = jnp.dot(
        lax.all_gather(activated, ("section", "tensor"), axis=0, tiled=True),
        w_down,
        preferred_element_type=jnp.float32,
    )
    ffn_out = lax.psum_scatter(
        partial_down.astype(jnp.bfloat16), "dp", scatter_dimension=0, tiled=True
    ).astype(jnp.float32)
    return (resid_mid.astype(jnp.float32) + ffn_out).astype(jnp.bfloat16)


def solution(mesh):
    return jax.shard_map(
        per_device,
        mesh=mesh,
        in_specs=(
            P("dp", ("section", "tensor")),
            P("dp", None),
            P(),
            P(None, ("section", "tensor")),
            P(None, ("section", "tensor")),
            P(None, ("section", "tensor")),
            P(("section", "tensor"), None),
            P(),
            P(("section", "tensor"), "dp"),
            P("dp", ("section", "tensor")),
        ),
        out_specs=P("dp", ("section", "tensor")),
        check_vma=False,
    )
```

profile of v0, /device:TPU:0, one launch (start us, length us, event | category | flops | bytes accessed | tf_op | source)
XLA Modules:
  0.0 492.6 jit_solution(8370720796275052697)
XLA Ops:
  6.5 0.0 copy-start
  6.5 0.0 copy-start.7
  6.5 0.0 all-gather.4.cloned.1.call-start
  6.5 0.7 all-gather.4.cloned.1.call-update
  7.3 0.0 all-reduce.2.cloned.1.call-start
  7.3 0.9 fusion.18
  8.2 40.8 %all-gather.4.cloned.1.call-done = bf16[256,8192]{1,0:T(8,128)(2,1)} async-done(((bf16[256,512]{1,0:T(8,128)(2,1)}), bf16[256,8192]{1,0:T(8,128)(2,1)}) %all-gather.4.cloned.1.call-update) | async-done | bytes 4194320 | tf_op jit(solution)/shard_map/all_gather | solution.py:23
  49.0 0.0 copy-start.3
  49.0 3.5 convert_reduce_fusion
  52.5 0.0 copy-done.7
  52.5 0.0 copy-done.3
  52.5 0.0 copy-start.5
  52.5 1.8 fusion.3
  54.3 0.4 copy-done.5
  54.7 0.0 copy-start.2
  54.7 0.0 copy-start.6
  54.7 1.8 convolution_convert_fusion.4
  56.6 0.3 copy-done.2
  56.9 1.6 copy-done.6
  58.4 1.8 convolution_convert_fusion.5
  60.3 0.4 fusion.23
  60.7 0.3 fusion.8
  60.9 5.2 %convolution_convert_fusion.6 = bf16[256,256]{0,1:T(8,128)(2,1)S(1)} fusion(bf16[256,8192]{1,0:T(8,128)(2,1)} %copy-done.2, bf16[8192,256]{1,0:T(8,128)(2,1)} %param.15), kind=kOutput, calls=%fused_computation.26 | convolution fusion | flops 1073807360 | bytes 8519680 | tf_op jit(solution)/shard_map/dot_general | solution.py:28
  66.1 0.3 convolution_convert_fusion.3
  66.4 5.4 %convolution_convert_fusion = bf16[256,8192]{1,0:T(8,128)(2,1)} fusion(bf16[256,256]{0,1:T(8,128)(2,1)S(1)} %bitcast.30, bf16[256,8192]{1,0:T(8,128)(2,1)} %param.16), kind=kOutput, calls=%fused_computation.5 | convolution fusion | flops 1075838976 | bytes 8519680 | tf_op jit(solution)/shard_map/dot_general | solution.py:46
  71.9 0.0 all-reduce.2.cloned.1.call-update
  71.9 0.2 all-gather.6.cloned.1.call-start
  72.1 0.8 dynamic-slice
  72.9 128.7 %all-reduce.2.cloned.1.call-done = bf16[256,8192]{1,0:T(8,128)(2,1)} async-done(((bf16[256,8192]{1,0:T(8,128)(2,1)}), bf16[256,8192]{1,0:T(8,128)(2,1)}) %all-reduce.2.cloned.1.call-update) | async-done | bytes 4194320 | tf_op jit(solution)/shard_map/psum | solution.py:47
  201.6 4.6 convert_reduce_fusion.1
  206.2 0.0 copy-start.4
  206.2 1.0 convert_element_type.73
  207.2 1.0 copy-done.4
  208.2 0.9 fusion.17
  209.0 0.0 all-gather.6.cloned.1.call-update
  209.1 0.0 reduce-scatter.3.cloned.1.call-start
  209.1 54.6 %all-gather.6.cloned.1.call-done = bf16[2048,512]{1,0:T(8,128)(2,1)} async-done(((bf16[256,512]{1,0:T(8,128)(2,1)}), bf16[2048,512]{1,0:T(8,128)(2,1)}) %all-gather.6.cloned.1.call-update) | async-done | bytes 2097168 | tf_op jit(solution)/shard_map/all_gather | solution.py:52
  263.7 0.0 copy-done
  263.7 8.3 %convolution_convert_fusion.1 = bf16[2048,2048]{1,0:T(8,128)(2,1)} fusion(bf16[2048,512]{1,0:T(8,128)(2,1)} %all-gather.6.cloned.1.call-done, bf16[512,2048]{1,0:T(8,128)(2,1)S(1)} %copy-done), kind=kOutput, calls=%fused_computation.12 | convolution fusion | flops 4299161600 | bytes 12582912 | tf_op jit(solution)/shard_map/dot_general | solution.py:54
  272.0 0.0 reduce-scatter.3.cloned.1.call-update
  272.0 0.0 all-gather.8.cloned.1.call-start
  272.1 73.0 %reduce-scatter.3.cloned.1.call-done = bf16[128,2048]{1,0:T(8,128)(2,1)} async-done(((bf16[2048,2048]{1,0:T(8,128)(2,1)}), bf16[128,2048]{1,0:T(8,128)(2,1)}) %reduce-scatter.3.cloned.1.call-update) | async-done | bytes 524304 | tf_op jit(solution)/shard_map/reduce_scatter | solution.py:53
  345.1 2.2 fusion.14
  347.4 0.0 all-gather.8.cloned.1.call-update
  347.4 0.0 reduce-scatter.5.cloned.1.call-start
  347.5 50.4 %all-gather.8.cloned.1.call-done = bf16[2048,2048]{1,0:T(8,128)(2,1)} async-done(((bf16[128,2048]{1,0:T(8,128)(2,1)}), bf16[2048,2048]{1,0:T(8,128)(2,1)}) %all-gather.8.cloned.1.call-update) | async-done | bytes 8388624 | tf_op jit(solution)/shard_map/all_gather | solution.py:61
  397.9 0.0 copy-start.1
  397.9 10.0 %convolution_convert_fusion.2 = bf16[2048,512]{1,0:T(8,128)(2,1)} fusion(bf16[2048,2048]{1,0:T(8,128)(2,1)} %all-gather.8.cloned.1.call-done, bf16[2048,512]{1,0:T(8,128)(2,1)} %param.19), kind=kOutput, calls=%fused_computation.14 | convolution fusion | flops 4296015872 | bytes 12582912 | tf_op jit(solution)/shard_map/dot_general | solution.py:60
  407.9 0.0 reduce-scatter.5.cloned.1.call-update
  407.9 76.0 %reduce-scatter.5.cloned.1.call-done = bf16[256,512]{1,0:T(8,128)(2,1)} async-done(((bf16[2048,512]{1,0:T(8,128)(2,1)}), bf16[256,512]{1,0:T(8,128)(2,1)}) %reduce-scatter.5.cloned.1.call-update) | async-done | bytes 262160 | tf_op jit(solution)/shard_map/reduce_scatter | solution.py:65
  484.0 1.8 add_convert_fusion
  485.8 0.0 copy-done.1
  (2 shorter events, 0.0 us)
Async XLA Ops:
  6.5 257.2 %copy-start = (bf16[512,2048]{1,0:T(8,128)(2,1)S(1)}, bf16[512,2048]{1,0:T(8,128)(2,1)}, u32[]{:S(2)}) copy-start(bf16[512,2048]{1,0:T(8,128)(2,1)} %param.18) | copy-start | bytes 6291460
  6.5 46.0 %copy-start.7 = (f32[8192]{0:T(1024)S(1)}, f32[8192]{0:T(1024)}, u32[]{:S(2)}) copy-start(f32[8192]{0:T(1024)} %param.12) | copy-start | bytes 98308
  6.5 42.4 %all-gather.4.cloned.1.call-start = ((), (), s32[]{:S(2)}) async-start(), calls=%async_computation.2 | async-start | bytes 4456448 | tf_op jit(solution)/shard_map/all_gather | solution.py:23
  7.3 194.3 %all-reduce.2.cloned.1.call-start = ((), (), s32[]{:S(2)}) async-start(), calls=%async_computation.3 | async-start | bytes 8388608 | tf_op jit(solution)/shard_map/psum | solution.py:47
  49.0 3.6 copy-start.3
  52.5 2.2 copy-start.5
  54.7 2.1 copy-start.2
  54.7 3.7 copy-start.6
  71.9 191.8 %all-gather.6.cloned.1.call-start = ((), (), s32[]{:S(2)}) async-start(), calls=%async_computation.4 | async-start | bytes 2359296 | tf_op jit(solution)/shard_map/all_gather | solution.py:52
  206.2 2.0 copy-start.4
  209.1 136.1 %reduce-scatter.3.cloned.1.call-start = ((), (), s32[]{:S(2)}) async-start(), calls=%async_computation.5 | async-start | bytes 8912896 | tf_op jit(solution)/shard_map/reduce_scatter | solution.py:53
  272.0 125.8 %all-gather.8.cloned.1.call-start = ((), (), s32[]{:S(2)}) async-start(), calls=%async_computation.6 | async-start | bytes 8912896 | tf_op jit(solution)/shard_map/all_gather | solution.py:61
  347.4 136.6 %reduce-scatter.5.cloned.1.call-start = ((), (), s32[]{:S(2)}) async-start(), calls=%async_computation.7 | async-start | bytes 2359296 | tf_op jit(solution)/shard_map/reduce_scatter | solution.py:65
  397.9 87.9 %copy-start.1 = (bf16[512,2048]{1,0:T(8,128)(2,1)S(1)}, bf16[512,2048]{1,0:T(8,128)(2,1)}, u32[]{:S(2)}) copy-start(bf16[512,2048]{1,0:T(8,128)(2,1)} %param.18) | copy-start | bytes 6291460
Sparse Core Ops, SparseCore 0:
  9.0 39.8 all-gather.3
  72.0 129.5 all-reduce.1
  209.2 54.4 all-gather.5
  272.2 72.9 reduce-scatter.2
  347.5 50.3 all-gather.7
  408.0 75.8 reduce-scatter.4
where the time goes:
time: 493 us
  waiting for transfers between devices  424 us (86%)
  matrix products  33.5 us (7%)
  other arithmetic  16.6 us (3%)
  between operations  13.6 us (3%)
    psum x1, waiting for transfers between devices, per_device(): lax.psum(partial_out.astype(jnp.bfloat16), ('section', 'tensor'))  129 us
    reduce_scatter x1, waiting for transfers between devices, per_device(): lax.psum_scatter(partial_down.astype(jnp.bfloat16), 'dp', scatter_dimensi...  76 us
    reduce_scatter x1, waiting for transfers between devices, per_device(): lax.psum_scatter(jnp.dot(gathered, w_up, preferred_element_type=jnp.float...  73 us
    all_gather x1, waiting for transfers between devices, per_device(): gathered = lax.all_gather(normed_ffn, 'dp', axis=0, tiled=True)  54.6 us
    all_gather x1, waiting for transfers between devices, per_device(): lax.all_gather(activated, ('section', 'tensor'), axis=0, tiled=True)  50.4 us
    all_gather x1, waiting for transfers between devices, per_device(): whole = lax.all_gather(tokens, ('section', 'tensor'), axis=1, tiled=True)  40.8 us
    dot_general x1, matrix products, per_device(): jnp.dot(lax.all_gather(activated, ('section', 'tensor'), axis=0, tiled=Tr...  9.99 us
  transfers between devices with their start and end apart: 6, of which 6 were waited for; matrix products, arithmetic and copies ran while one was open for 0% of the time, Pallas kernels for 0%

commit v1 on v0

--- a/solution.py
+++ b/solution.py
@@ -44,7 +44,9 @@
     context = jnp.einsum("hqk,khd->qhd", probs, value, preferred_element_type=jnp.float32)
     context = context.astype(jnp.bfloat16).reshape(tok_rows, local_heads * HD)
     partial_out = jnp.dot(context, w_output, preferred_element_type=jnp.float32)
-    summed = lax.psum(partial_out.astype(jnp.bfloat16), ("section", "tensor")).astype(jnp.float32)
+    summed = lax.psum(lax.psum(partial_out.astype(jnp.bfloat16), "section"), "tensor").astype(
+        jnp.float32
+    )
     resid_full = (whole.astype(jnp.float32) + summed).astype(jnp.bfloat16)
     normed_full = layer_norm(resid_full.astype(jnp.float32), gain_ffn).astype(jnp.bfloat16)
     normed_ffn = lax.dynamic_slice_in_dim(normed_full, first_col, share, 1)

time: 493 us -> 554 us (1.12)
  waiting for transfers between devices: 424 us -> 485 us
    psum x1 -> x2, waiting for transfers between devices: 129 us -> 190 us  [the longest x1 115 us: per_device(): lax.psum(partial_out.astype(jnp.bfloat16), 'section')]
  transfers between devices with their start and end apart: 6 -> 7, of which waited for: 6 -> 7; matrix products, arithmetic and copies ran while one was open for 0% -> 0% of each run, Pallas kernels for 0% -> 0%
where the time goes in v1:
time: 554 us; the launch traced here: 553 us
  waiting for transfers between devices  485 us (88%)
  matrix products  33.5 us (6%)
  other arithmetic  16.6 us (3%)
  between operations  13.6 us (2%)
    psum x1, waiting for transfers between devices, per_device(): lax.psum(partial_out.astype(jnp.bfloat16), 'section')  115 us
    reduce_scatter x1, waiting for transfers between devices, per_device(): lax.psum_scatter(partial_down.astype(jnp.bfloat16), 'dp', scatter_dimensi...  76.1 us
    psum x1, waiting for transfers between devices, per_device(): lax.psum(lax.psum(partial_out.astype(jnp.bfloat16), 'section'), 'tensor')  75.4 us
    reduce_scatter x1, waiting for transfers between devices, per_device(): lax.psum_scatter(jnp.dot(gathered, w_up, preferred_element_type=jnp.float...  73 us
    all_gather x1, waiting for transfers between devices, per_device(): gathered = lax.all_gather(normed_ffn, 'dp', axis=0, tiled=True)  53.9 us
    all_gather x1, waiting for transfers between devices, per_device(): lax.all_gather(activated, ('section', 'tensor'), axis=0, tiled=True)  50.4 us
    all_gather x1, waiting for transfers between devices, per_device(): whole = lax.all_gather(tokens, ('section', 'tensor'), axis=1, tiled=True)  40.8 us
  transfers between devices with their start and end apart: 7, of which 7 were waited for; matrix products, arithmetic and copies ran while one was open for 0% of the time, Pallas kernels for 0%

profile of v1, /device:TPU:0, one launch (start us, length us, event | category | flops | bytes accessed | tf_op | source)
XLA Modules:
  0.0 553.2 jit_solution(8000734959263812832)
XLA Ops:
  6.5 0.0 copy-start
  6.5 0.0 copy-start.7
  6.5 0.0 all-gather.4.cloned.1.call-start
  6.5 0.7 all-gather.4.cloned.1.call-update
  7.3 0.0 all-reduce.3.cloned.1.call-start
  7.3 0.9 fusion.18
  8.2 40.8 %all-gather.4.cloned.1.call-done = bf16[256,8192]{1,0:T(8,128)(2,1)} async-done(((bf16[256,512]{1,0:T(8,128)(2,1)}), bf16[256,8192]{1,0:T(8,128)(2,1)}) %all-gather.4.cloned.1.call-update) | async-done | bytes 4194320 | tf_op jit(solution)/shard_map/all_gather | solution.py:23
  49.0 0.0 copy-start.3
  49.0 3.5 convert_reduce_fusion
  52.5 0.0 copy-done.7
  52.5 0.0 copy-done.3
  52.5 0.0 copy-start.5
  52.5 1.8 fusion.3
  54.3 0.4 copy-done.5
  54.7 0.0 copy-start.2
  54.7 0.0 copy-start.6
  54.7 1.8 convolution_convert_fusion.4
  56.6 0.3 copy-done.2
  56.9 1.6 copy-done.6
  58.4 1.8 convolution_convert_fusion.5
  60.3 0.4 fusion.23
  60.7 0.3 fusion.8
  60.9 5.2 convolution_convert_fusion.6
  66.1 0.3 convolution_convert_fusion.3
  66.4 5.4 convolution_convert_fusion
  71.9 0.0 all-reduce.3.cloned.1.call-update
  71.9 0.0 all-reduce.5.cloned.1.call-start
  71.9 114.5 %all-reduce.3.cloned.1.call-done = bf16[256,8192]{1,0:T(8,128)(2,1)} async-done(((bf16[256,8192]{1,0:T(8,128)(2,1)}), bf16[256,8192]{1,0:T(8,128)(2,1)}) %all-reduce.3.cloned.1.call-update) | async-done | bytes 4194320 | tf_op jit(solution)/shard_map/psum | solution.py:47
  186.5 0.0 all-reduce.5.cloned.1.call-update
  186.5 0.2 all-gather.6.cloned.1.call-start
  186.7 0.8 dynamic-slice
  187.5 75.4 %all-reduce.5.cloned.1.call-done = bf16[256,8192]{1,0:T(8,128)(2,1)} async-done(((bf16[256,8192]{1,0:T(8,128)(2,1)}), bf16[256,8192]{1,0:T(8,128)(2,1)}) %all-reduce.5.cloned.1.call-update) | async-done | bytes 4194320 | tf_op jit(solution)/shard_map/psum | solution.py:47
  262.9 4.6 convert_reduce_fusion.1
  267.5 0.0 copy-start.4
  267.5 1.0 convert_element_type.73
  268.5 1.0 copy-done.4
  269.5 0.9 fusion.17
  270.3 0.0 all-gather.6.cloned.1.call-update
  270.4 0.0 reduce-scatter.3.cloned.1.call-start
  270.4 53.9 %all-gather.6.cloned.1.call-done = bf16[2048,512]{1,0:T(8,128)(2,1)} async-done(((bf16[256,512]{1,0:T(8,128)(2,1)}), bf16[2048,512]{1,0:T(8,128)(2,1)}) %all-gather.6.cloned.1.call-update) | async-done | bytes 2097168 | tf_op jit(solution)/shard_map/all_gather | solution.py:54
  324.3 0.0 copy-done
  324.3 8.3 %convolution_convert_fusion.1 = bf16[2048,2048]{1,0:T(8,128)(2,1)} fusion(bf16[2048,512]{1,0:T(8,128)(2,1)} %all-gather.6.cloned.1.call-done, bf16[512,2048]{1,0:T(8,128)(2,1)S(1)} %copy-done), kind=kOutput, calls=%fused_computation.12 | convolution fusion | flops 4299161600 | bytes 12582912 | tf_op jit(solution)/shard_map/dot_general | solution.py:56
  332.6 0.0 reduce-scatter.3.cloned.1.call-update
  332.6 0.0 all-gather.8.cloned.1.call-start
  332.7 73.0 %reduce-scatter.3.cloned.1.call-done = bf16[128,2048]{1,0:T(8,128)(2,1)} async-done(((bf16[2048,2048]{1,0:T(8,128)(2,1)}), bf16[128,2048]{1,0:T(8,128)(2,1)}) %reduce-scatter.3.cloned.1.call-update) | async-done | bytes 524304 | tf_op jit(solution)/shard_map/reduce_scatter | solution.py:55
  405.7 2.2 fusion.14
  407.9 0.0 all-gather.8.cloned.1.call-update
  408.0 0.0 reduce-scatter.5.cloned.1.call-start
  408.0 50.4 %all-gather.8.cloned.1.call-done = bf16[2048,2048]{1,0:T(8,128)(2,1)} async-done(((bf16[128,2048]{1,0:T(8,128)(2,1)}), bf16[2048,2048]{1,0:T(8,128)(2,1)}) %all-gather.8.cloned.1.call-update) | async-done | bytes 8388624 | tf_op jit(solution)/shard_map/all_gather | solution.py:63
  458.5 0.0 copy-start.1
  458.5 10.0 %convolution_convert_fusion.2 = bf16[2048,512]{1,0:T(8,128)(2,1)} fusion(bf16[2048,2048]{1,0:T(8,128)(2,1)} %all-gather.8.cloned.1.call-done, bf16[2048,512]{1,0:T(8,128)(2,1)} %param.19), kind=kOutput, calls=%fused_computation.14 | convolution fusion | flops 4296015872 | bytes 12582912 | tf_op jit(solution)/shard_map/dot_general | solution.py:62
  468.5 0.0 reduce-scatter.5.cloned.1.call-update
  468.5 76.1 %reduce-scatter.5.cloned.1.call-done = bf16[256,512]{1,0:T(8,128)(2,1)} async-done(((bf16[2048,512]{1,0:T(8,128)(2,1)}), bf16[256,512]{1,0:T(8,128)(2,1)}) %reduce-scatter.5.cloned.1.call-update) | async-done | bytes 262160 | tf_op jit(solution)/shard_map/reduce_scatter | solution.py:67
  544.5 1.8 add_convert_fusion
  546.3 0.0 copy-done.1
  (2 shorter events, 0.0 us)
Async XLA Ops:
  6.5 317.8 %copy-start = (bf16[512,2048]{1,0:T(8,128)(2,1)S(1)}, bf16[512,2048]{1,0:T(8,128)(2,1)}, u32[]{:S(2)}) copy-start(bf16[512,2048]{1,0:T(8,128)(2,1)} %param.18) | copy-start | bytes 6291460
  6.5 46.0 %copy-start.7 = (f32[8192]{0:T(1024)S(1)}, f32[8192]{0:T(1024)}, u32[]{:S(2)}) copy-start(f32[8192]{0:T(1024)} %param.12) | copy-start | bytes 98308
  6.5 42.4 %all-gather.4.cloned.1.call-start = ((), (), s32[]{:S(2)}) async-start(), calls=%async_computation.2 | async-start | bytes 4456448 | tf_op jit(solution)/shard_map/all_gather | solution.py:23
  7.3 179.2 %all-reduce.3.cloned.1.call-start = ((), (), s32[]{:S(2)}) async-start(), calls=%async_computation.3 | async-start | bytes 8388608 | tf_op jit(solution)/shard_map/psum | solution.py:47
  49.0 3.6 copy-start.3
  52.5 2.2 copy-start.5
  54.7 2.1 copy-start.2
  54.7 3.7 copy-start.6
  71.9 191.0 %all-reduce.5.cloned.1.call-start = ((), (), s32[]{:S(2)}) async-start(), calls=%async_computation.4 | async-start | bytes 8388608 | tf_op jit(solution)/shard_map/psum | solution.py:47
  186.5 137.8 %all-gather.6.cloned.1.call-start = ((), (), s32[]{:S(2)}) async-start(), calls=%async_computation.5 | async-start | bytes 2359296 | tf_op jit(solution)/shard_map/all_gather | solution.py:54
  267.5 2.0 copy-start.4
  270.4 135.3 %reduce-scatter.3.cloned.1.call-start = ((), (), s32[]{:S(2)}) async-start(), calls=%async_computation.6 | async-start | bytes 8912896 | tf_op jit(solution)/shard_map/reduce_scatter | solution.py:55
  332.6 125.8 %all-gather.8.cloned.1.call-start = ((), (), s32[]{:S(2)}) async-start(), calls=%async_computation.7 | async-start | bytes 8912896 | tf_op jit(solution)/shard_map/all_gather | solution.py:63
  408.0 136.6 %reduce-scatter.5.cloned.1.call-start = ((), (), s32[]{:S(2)}) async-start(), calls=%async_computation.8 | async-start | bytes 2359296 | tf_op jit(solution)/shard_map/reduce_scatter | solution.py:67
  458.5 87.9 %copy-start.1 = (bf16[512,2048]{1,0:T(8,128)(2,1)S(1)}, bf16[512,2048]{1,0:T(8,128)(2,1)}, u32[]{:S(2)}) copy-start(bf16[512,2048]{1,0:T(8,128)(2,1)} %param.18) | copy-start | bytes 6291460
Sparse Core Ops, SparseCore 0:
  9.0 39.8 all-gather.3
  72.0 114.3 all-reduce.2
  189.0 73.9 all-reduce.4
  270.5 53.7 all-gather.5
  332.7 72.9 reduce-scatter.2
  408.1 50.3 all-gather.7
  468.6 75.9 reduce-scatter.4
